TPU v7x, 128 devices: a whole 4x4x4 slice. The times are simulated.
128 devices in a mesh: tm: 4 (over y_lo, core), tile: 32 (over y_hi, z, x).
Axes of the slice: x: 4, y: 4 (y_hi: 2, y_lo: 2; y = y_hi * 2 + y_lo), z: 4, core: 2. Of those that a mesh axis runs over, the one named last changes fastest.
Arguments:
- latent_grad: bfloat16 [32, 160, 4096], P(None, 'tile', 'tm'), may hold values from -6 to 6
- section_input: bfloat16 [32, 160, 256, 512], P('tm', None, 'tile'), may hold values from -6 to 6
- kernel: bfloat16 [512, 432], replicated, may hold values from -0.3125 to 0.3125
Outputs:
- input_grad: bfloat16 [32, 160, 256, 512], P('tm', None, 'tile')
- kernel_grad: float32 [512, 432], P('tile')
All inputs are finite; a program needn't handle non-finite values.
Results may differ from a plain program's by a relative error of at most 0.0029.
Values may be sent and summed in bfloat16 or wider, within the bound.
A program may use at most 128 MiB of HBM per device.

v0:
```python
import functools
import math

import jax
import jax.numpy as jnp
from jax import lax
from jax.experimental import pallas as pl
from jax.experimental.pallas import tpu as pltpu
from jax.sharding import PartitionSpec as P

MESH = pl.DeviceIdType.MESH
F32, BF16 = jnp.float32, jnp.bfloat16
LANES = 128
OUT = 16
STRIP = 8
FRAMES = 8
ROWS = 5
FIRST = 5
SECOND = 4
EARLY = 4
CORES = 2
WINDOW = 3


def lane_of(shape, axis):
    return lax.broadcasted_iota(jnp.int32, shape, axis)


def aligned(index, size):
    return pl.ds(pl.multiple_of(index * size, size), size)


def turned(value, shift, axis):
    shift %= value.shape[axis]
    return pltpu.roll(value, shift, axis) if shift else value


def wrapped(index, size):
    return jnp.where(index >= size, index - size, index)


def strip_halo(left, right):
    lane = lane_of((1, LANES), 1)
    rows = []
    for i in range(ROWS):
        value = jnp.zeros((FRAMES, LANES), F32)
        if right is not None:
            value = jnp.where(lane >= LANES - OUT, right[i], value)
        if left is not None:
            value = jnp.where(lane < OUT, left[i], value)
        rows.append(turned(value, OUT + 2 * OUT * i, 1))
    return rows[0] + rows[1] + rows[2] + rows[3], rows[4]


def later_halo(first, second):
    row = lane_of((FRAMES, 1), 0)
    value = jnp.where(row < 6, turned(second, 4, 0), 0.0)
    return jnp.where(row < 2, 0.0, jnp.where(row < 4, turned(first, 2, 0), value))


def whole(
    n_tm, n_tile, scale, grad_hbm, x_ref, kernel_hbm, out_ref, kgrad_ref,
    grad_ref, kernel_ref, msg, msg_2, emsg, recv, recv_2, edge, act, slope, field, halo, vee, cols, cols_t, last, last_t,
    weights, acc, part, mine, mine_half, pieces, sums, quads, in_sem, sems,
):
    frames, height, width, cin = out_ref.shape
    wide, count = frames + 2, height * width
    tm, tile = lax.axis_index("tm"), lax.axis_index("tile")
    strips = n_tile // n_tm
    block = tile // strips
    place_in_block = lax.rem(tile, strips)
    from_left = jnp.logical_and(place_in_block == 0, block > 0)
    from_right = jnp.logical_and(place_in_block == strips - 1, block < n_tm - 1)
    has_edge = jnp.logical_or(from_left, from_right)
    edge_block = jnp.where(place_in_block == 0, block - 1, block + 1)
    messages = n_tm * strips
    send_main, send_edge, recv_main, recv_edge = (sems.at[i] for i in range(4))
    swap_send, swap_recv, piece_send, piece_recv = (sems.at[i] for i in range(4, 8))
    send_2, recv_main_2 = sems.at[10], sems.at[11]
    row_send, row_recv = sems.at[12], sems.at[13]
    core, y_lo = lax.rem(tm, CORES), tm // CORES
    groups = n_tile // CORES
    y_hi, spot = tile // groups, lax.rem(tile, groups)
    partner = tm + 1 - 2 * core
    level = y_hi * CORES + y_lo
    owner_tile = core * groups + spot

    def is_me(target_tm, target_tile):
        return jnp.logical_and(target_tm == tm, target_tile == tile)

    grad_copy = pltpu.make_async_copy(grad_hbm, grad_ref, sems.at[8])
    kernel_copy = pltpu.make_async_copy(kernel_hbm, kernel_ref, sems.at[9])
    grad_copy.start()
    kernel_copy.start()

    def fetch(t):
        return pltpu.make_async_copy(x_ref.at[t], out_ref.at[t], in_sem.at[t])

    for t in range(frames):
        fetch(t).start()

    barrier = pltpu.get_barrier_semaphore()

    def hail(target_tm, target_tile):
        pl.semaphore_signal(barrier, inc=1, device_id=(target_tm, target_tile), device_id_type=MESH)

    for k in range(1, n_tile):
        hail(block, wrapped(tile + k, n_tile))

    @pl.when(block != tm)
    def _():
        hail(block, tile)

    @pl.when(has_edge)
    def _():
        for k in range(1, n_tile):
            hail(edge_block, wrapped(tile + k, n_tile))

        @pl.when(edge_block != tm)
        def _():
            hail(edge_block, tile)

    hail(partner, tile)
    for k in range(1, groups):
        hail(tm, y_hi * groups + wrapped(spot + k, groups))
    for k in range(n_tm):
        source = (k % CORES) * CORES + y_hi, (k // CORES) * groups + spot

        @pl.when(jnp.logical_not(is_me(*source)))
        def _():
            hail(*source)

    r, c = lane_of((LANES, LANES), 0), lane_of((LANES, LANES), 1)
    same = jnp.logical_and(r // OUT + c // OUT == STRIP - 1, lax.rem(r, OUT) == lax.rem(c, OUT))
    flip = jnp.where(same, 1.0, 0.0).astype(BF16)
    row = lane_of((FRAMES, 1), 0)
    nothing = jnp.zeros((FRAMES, LANES), F32)
    grad_copy.wait()
    flipped, halos = [], []
    for t in range(n_tm):
        rows = grad_ref[:, t].astype(F32).reshape(ROWS * FRAMES, strips * LANES).astype(BF16)
        here = [
            jnp.dot(rows[:, s * LANES : (s + 1) * LANES], flip, preferred_element_type=F32)
            .reshape(ROWS, FRAMES, LANES)
            for s in range(strips)
        ]
        flipped.append(here)
        padded = [None, None] + here + [None, None]
        halos.append([strip_halo(padded[s], padded[s + 2]) for s in range(strips + 2)])
    later = []
    for t in range(n_tm):
        later.append([
            nothing if t + 1 == n_tm else later_halo(*halos[t + 1][s]) for s in range(strips + 2)
        ])
        for s in range(strips):
            here = flipped[t][s]
            tiles = [
                jnp.where(row < EARLY, here[0], turned(here[1], EARLY, 0)),
                jnp.where(row < EARLY, here[2], turned(here[3], EARLY, 0)),
                here[4], *halos[t][s + 1],
            ]
            for i, value in enumerate(tiles):
                msg[t, s, i] = value.astype(BF16)
        for side, s in ((0, strips + 1), (1, 0)):
            for i, value in enumerate([*halos[t][s], later[t][s]]):
                emsg[side, t, i] = value.astype(BF16)

    self_main = (block == tm).astype(jnp.int32)
    to_right, to_left = tm < n_tm - 1, tm > 0
    right_tile, left_tile = (tm + 1) * strips, tm * strips - 1
    self_edge = (
        jnp.logical_and(to_right, tile == right_tile).astype(jnp.int32)
        + jnp.logical_and(to_left, tile == left_tile).astype(jnp.int32)
    )
    edges_out = n_tm * (to_right.astype(jnp.int32) + to_left.astype(jnp.int32))
    self_owner = (core == y_hi).astype(jnp.int32)
    exchange_out = messages - self_main + edges_out - self_edge
    pl.semaphore_wait(barrier, exchange_out + 1 + groups - 1 + n_tm - self_owner)

    def send(source, target, send_sem, recv_sem, target_tm, target_tile):
        own = is_me(target_tm, target_tile)

        @pl.when(jnp.logical_not(own))
        def _():
            pltpu.make_async_remote_copy(
                src_ref=source, dst_ref=target, send_sem=send_sem, recv_sem=recv_sem,
                device_id=(target_tm, target_tile), device_id_type=MESH,
            ).start()

        @pl.when(own)
        def _():
            pltpu.make_async_copy(source, target, recv_sem).start()

    def send_edges(t, _):
        @pl.when(to_right)
        def _():
            send(emsg.at[0, t], edge.at[tile], send_edge, recv_edge, t, right_tile)

        @pl.when(to_left)
        def _():
            send(emsg.at[1, t], edge.at[tile], send_edge, recv_edge, t, left_tile)

        return 0

    def send_all(source, target, send_sem, recv_sem):
        for k in range(messages):
            t, s = wrapped(tm + k // strips, n_tm), wrapped(place_in_block + k % strips, strips)
            if k == 0:
                send(source.at[t, s], target.at[tile], send_sem, recv_sem, t, tm * strips + s)
            else:
                pltpu.make_async_remote_copy(
                    src_ref=source.at[t, s], dst_ref=target.at[tile], send_sem=send_sem, recv_sem=recv_sem,
                    device_id=(t, tm * strips + s), device_id_type=MESH,
                ).start()

    lax.fori_loop(0, n_tm, send_edges, 0)
    send_all(msg, recv, send_main, recv_main)

    for t in range(n_tm):
        for s in range(strips):
            here, rest = flipped[t][s], later[t][s + 1]
            if t + 1 < n_tm:
                nxt = flipped[t + 1][s]
                late = jnp.where(row < 6, turned(nxt[2], 4, 0), turned(nxt[3], 6, 0))
                late = jnp.where(row < 2, nxt[0], jnp.where(row < 4, turned(nxt[1], 2, 0), late))
                rest = jnp.where(row < 2, nxt[4], rest)
            else:
                late = nothing
            tiles = [
                jnp.where(row < EARLY, turned(here[0], EARLY, 0), here[1]),
                jnp.where(row < EARLY, turned(here[2], EARLY, 0), here[3]),
                late, rest,
            ]
            for i, value in enumerate(tiles):
                msg_2[t, s, i] = value.astype(BF16)

    kernel_copy.wait()
    weights[...] = jnp.zeros(weights.shape, BF16)
    for kt in range(3):
        taps = kernel_ref[9 * kt * OUT : 9 * (kt + 1) * OUT, :]
        taps = (0.5 * taps.astype(F32)).astype(BF16)
        weights[kt * LANES : (kt + 1) * LANES, :] = taps[:LANES]
        weights[3 * LANES + kt * OUT : 3 * LANES + (kt + 1) * OUT, :] = taps[LANES:]

    step = 8

    def silu_frame(t, _):
        fetch(t).wait()

        def silu_rows(r, _):
            half_x = 0.5 * out_ref[t, pl.ds(r * step, step)].astype(F32).reshape(step * width, cin)
            u = jnp.tanh(half_x)
            more = 1.0 + u
            value = half_x * more
            rows = aligned(r, step * width)
            act[t, rows, :] = value.astype(BF16)
            slope[t, rows, :] = more + value * (1.0 - u)
            return 0

        lax.fori_loop(0, height // step, silu_rows, 0, unroll=4)
        return 0

    lax.fori_loop(0, EARLY, silu_frame, 0)
    send_all(msg_2, recv_2, send_2, recv_main_2)
    lax.fori_loop(EARLY, frames, silu_frame, 0)

    @pl.when(jnp.logical_not(has_edge))
    def _():
        edge[...] = jnp.zeros(edge.shape, BF16)

    @pl.when(has_edge)
    def _():
        pltpu.make_async_copy(edge, edge, recv_edge).wait()

    pltpu.make_async_copy(recv, recv, recv_main).wait()

    def unpack(b, _):
        tiles = [recv[b, i].astype(F32) for i in range(FIRST)]
        beside = tiles[3] + edge[b, 0].astype(F32)
        beside_4 = tiles[4] + edge[b, 1].astype(F32)
        for i in range(ROWS):
            at = b * ROWS + i
            field[at, 0:FRAMES] = turned(tiles[i // 2], EARLY * (i % 2), 0)
            halo[at, 0:FRAMES] = turned(beside if i < 4 else beside_4, -OUT - 2 * OUT * i, 1)
        return 0

    def unpack_2(b, _):
        tiles = [recv_2[b, i].astype(F32) for i in range(SECOND)]
        late = tiles[3] + edge[b, 2].astype(F32)
        for i in range(ROWS):
            at = b * ROWS + i
            if i < 4:
                field[at, EARLY:FRAMES] = turned(tiles[i // 2], EARLY * (1 - i % 2), 0)[EARLY:]
            field[at, FRAMES:] = turned(tiles[2], -2 * i, 0) if i < 4 else late
            halo[at, FRAMES:] = turned(turned(late, -2 if i < 4 else -4, 0), -OUT - 2 * OUT * i, 1)
        return 0

    lax.fori_loop(0, n_tile, unpack, 0, unroll=4)

    lane3, col3 = lane_of((1, width, LANES), 2), lane_of((1, width, LANES), 1)
    outside = jnp.logical_or(
        jnp.logical_and(col3 == 0, lane3 < OUT),
        jnp.logical_and(col3 == width - 1, lane3 >= LANES - OUT),
    )
    edge_rows = jnp.zeros((width, LANES), F32)
    group = 16
    for t in range(WINDOW):
        vee[t, 0:width, :] = edge_rows
        vee[t, (height + 1) * width : (height + 2) * width, :] = edge_rows

    lane2 = lane_of((1, LANES), 1)

    def tap(t, g, shift_rows, shift):
        at = pl.ds(pl.multiple_of((g * group + shift_rows) * width, width), group * width)
        return turned(vee[t % WINDOW, at, :].astype(BF16), shift, 1)

    acc[...] = jnp.zeros(acc.shape, F32)

    def add_frame(t):
        left = jnp.concatenate([cols_t[t * LANES : (t + 3) * LANES, :], last_t[t]], axis=0)
        acc[...] += jnp.dot(left, act[t], preferred_element_type=F32)

    for t in range(wide):
        if t == EARLY:
            pltpu.make_async_copy(recv_2, recv_2, recv_main_2).wait()
            lax.fori_loop(0, n_tile, unpack_2, 0, unroll=4)

        def spread(g, _, t=t):
            rows = pl.ds(g * group, group)
            main = jnp.broadcast_to(field[rows, t : t + 1, :], (group, width, LANES))
            side = jnp.broadcast_to(halo[rows, t : t + 1, :], (group, width, LANES))
            at = pl.ds(pl.multiple_of((g * group + 1) * width, width), group * width)
            values = jnp.where(outside, side, main).reshape(group * width, LANES)
            vee[t % WINDOW, at, :] = pltpu.roll(values, 0, 1, stride=OUT, stride_axis=0)
            return 0

        def fill(g, _, t=t):
            rows = aligned(g, group * width)
            s0, s1, s2 = tap(t, g, 2, 2 * OUT), tap(t, g, 1, 5 * OUT), tap(t, g, 0, 0)
            cols[t, rows, :] = jnp.where(lane2 < 3 * OUT, s0, jnp.where(lane2 < 6 * OUT, s1, s2))
            return 0

        def fill_last(g, _, t=t):
            rows = aligned(g, group * width)
            taps = [tap(t - 2 + kt, g, 0, kt * OUT) for kt in range(3)]
            value = jnp.where(lane2 < 3 * OUT, taps[2], jnp.zeros_like(taps[2]))
            last[t - 2, rows, :] = jnp.where(lane2 < OUT, taps[0], jnp.where(lane2 < 2 * OUT, taps[1], value))
            return 0

        lax.fori_loop(0, height // group, spread, 0, unroll=True)
        lax.fori_loop(0, height // group, fill, 0, unroll=True)
        cols_t[t * LANES : (t + 1) * LANES, :] = jnp.transpose(cols[t])
        if t >= 2:
            lax.fori_loop(0, height // group, fill_last, 0, unroll=True)
            last_t[t - 2] = jnp.transpose(last[t - 2])[0 : 3 * OUT]
        if t >= 3:
            add_frame(t - 3)
    add_frame(frames - 1)

    pieces_of_total = []
    for kt in range(3):
        pieces_of_total.append(acc[kt * LANES : (kt + 1) * LANES, :])
        pieces_of_total.append(acc[3 * LANES + kt * OUT : 3 * LANES + (kt + 1) * OUT, :])
    pieces_of_total.append(jnp.zeros((part.shape[1] - 27 * OUT, cin), F32))
    part[...] = jnp.transpose(jnp.concatenate(pieces_of_total, axis=0))

    chunk = 40

    def grad_frame(t, _):
        def grad_rows(r, _):
            rows = aligned(r, chunk * width)
            left = jnp.concatenate([cols[t + kt, rows, :] for kt in range(3)] + [last[t, rows, :]], axis=1)
            grad = jnp.dot(left, weights[...], preferred_element_type=F32) * slope[t, rows, :]
            out_ref[t, pl.ds(r * chunk, chunk)] = grad.reshape(chunk, width, cin).astype(BF16)
            return 0

        lax.fori_loop(0, height // chunk, grad_rows, 0, unroll=True)
        return 0

    def drain(source, sem):
        pltpu.make_async_copy(source, source, sem).wait()

    def drain_messages(source, sem):
        if n_tm > 1:
            drain(source.at[pl.ds(0, n_tm - 1)], sem)
        if strips > 1:
            drain(source.at[0, pl.ds(0, strips - 1)], sem)

        @pl.when(block != tm)
        def _():
            drain(source.at[0, 0], sem)

    drain_messages(msg, send_main)
    drain_messages(msg_2, send_2)

    def drain_edge(k, _):
        drain(emsg.at[0, 0], send_edge)
        return 0

    lax.fori_loop(0, edges_out - self_edge, drain_edge, 0)

    rows = mine.shape[0]
    share = rows // groups
    swap = pltpu.make_async_remote_copy(
        src_ref=part.at[aligned(1 - core, rows)], dst_ref=mine,
        send_sem=swap_send, recv_sem=swap_recv,
        device_id=(partner, tile), device_id_type=MESH,
    )
    swap.start()
    lax.fori_loop(0, SPLIT[0], grad_frame, 0)
    swap.wait()
    mine[...] += part[aligned(core, rows), :]

    mine_half[...] = mine[...].astype(BF16)

    for k in range(1, groups):
        g = wrapped(spot + k, groups)
        pltpu.make_async_remote_copy(
            src_ref=mine_half.at[aligned(g, share)], dst_ref=pieces.at[spot],
            send_sem=piece_send, recv_sem=piece_recv,
            device_id=(tm, y_hi * groups + g), device_id_type=MESH,
        ).start()
    pieces[spot] = mine_half[aligned(spot, share), :]
    lax.fori_loop(SPLIT[0], SPLIT[1], grad_frame, 0)
    others = pieces.at[pl.ds(0, groups - 1)]
    pltpu.make_async_copy(others, others, piece_recv).wait()
    sums[...] = jnp.sum(pieces[...].astype(F32), axis=0)

    for k in range(n_tm):
        send(sums, quads.at[level], row_send, row_recv, k, owner_tile)
    lax.fori_loop(SPLIT[1], frames, grad_frame, 0)
    pltpu.make_async_copy(quads, quads, row_recv).wait()

    drain(others, piece_send)
    drain(quads.at[pl.ds(0, n_tm - 1)], row_send)

    @pl.when(core != y_hi)
    def _():
        drain(sums, row_send)

    result = quads[0]
    for k in range(1, n_tm):
        result = result + quads[k]
    kgrad_ref[...] = (result * scale)[:, : kgrad_ref.shape[1]]


SPLIT = (1, 7)


def write_out(grad_ref, kgrad_ref, grad_out, kgrad_out, sem):
    frames, height = grad_ref.shape[:2]
    copies = [pltpu.make_async_copy(kgrad_ref, kgrad_out, sem.at[2 * frames])]
    for i in range(2 * frames):
        place = (i // 2, pl.ds((i % 2) * (height // 2), height // 2))
        copies.append(pltpu.make_async_copy(grad_ref.at[place], grad_out.at[place], sem.at[i]))
    for copy in copies:
        copy.start()
    for copy in copies:
        copy.wait()


def on_device(n_tm, n_tile, scale, latent_grad, section_input, kernel):
    frames, height, width, cin = section_input.shape
    taps = kernel.shape[1]
    strips = n_tile // n_tm
    banded = jnp.transpose(latent_grad, (1, 0, 2)).reshape(ROWS, n_tm, FRAMES, strips * LANES)
    wide, count = frames + 2, height * width
    rows, share, padded = cin // CORES, cin // n_tile, 4 * LANES
    vmem = pl.BlockSpec(memory_space=pltpu.VMEM)
    results = pl.pallas_call(
        functools.partial(whole, n_tm, n_tile, scale),
        out_shape=(
            pltpu.VMEM((frames, height, width, cin), BF16),
            pltpu.VMEM((share, taps), F32),
        ),
        in_specs=[pl.BlockSpec(memory_space=pl.ANY)] * 3,
        out_specs=(vmem, vmem),
        scratch_shapes=[
            pltpu.VMEM((ROWS, n_tm, FRAMES, strips * LANES), BF16),
            pltpu.VMEM((taps, cin), BF16),
            pltpu.VMEM((n_tm, strips, FIRST, FRAMES, LANES), BF16),
            pltpu.VMEM((n_tm, strips, SECOND, FRAMES, LANES), BF16),
            pltpu.VMEM((2, n_tm, 3, FRAMES, LANES), BF16),
            pltpu.VMEM((n_tile, FIRST, FRAMES, LANES), BF16),
            pltpu.VMEM((n_tile, SECOND, FRAMES, LANES), BF16),
            pltpu.VMEM((n_tile, 3, FRAMES, LANES), BF16),
            pltpu.VMEM((frames, count, cin), BF16),
            pltpu.VMEM((frames, count, cin), F32),
            pltpu.VMEM((height, 2 * FRAMES, LANES), F32),
            pltpu.VMEM((height, 2 * FRAMES, LANES), F32),
            pltpu.VMEM((WINDOW, (height + 2) * width, LANES), F32),
            pltpu.VMEM((wide, count, LANES), BF16),
            pltpu.VMEM((wide * LANES, count), BF16),
            pltpu.VMEM((frames, count, LANES), BF16),
            pltpu.VMEM((frames, 3 * OUT, count), BF16),
            pltpu.VMEM((padded, cin), BF16),
            pltpu.VMEM((27 * OUT, cin), F32),
            pltpu.VMEM((cin, padded), F32),
            pltpu.VMEM((rows, padded), F32),
            pltpu.VMEM((rows, padded), BF16),
            pltpu.VMEM((n_tile // CORES, share, padded), BF16),
            pltpu.VMEM((share, padded), F32),
            pltpu.VMEM((n_tm, share, padded), F32),
            pltpu.SemaphoreType.DMA((frames,)),
            pltpu.SemaphoreType.DMA((16,)),
        ],
        compiler_params=pltpu.CompilerParams(
            collective_id=0, has_side_effects=True, vmem_limit_bytes=VMEM_LIMIT
        ),
    )(banded, section_input, jnp.transpose(kernel))
    return pl.pallas_call(
        write_out,
        out_shape=(
            jax.ShapeDtypeStruct((frames, height, width, cin), BF16),
            jax.ShapeDtypeStruct((share, taps), F32),
        ),
        in_specs=[vmem, vmem],
        out_specs=[pl.BlockSpec(memory_space=pl.ANY)] * 2,
        scratch_shapes=[pltpu.SemaphoreType.DMA((2 * frames + 1,))],
    )(*results)


VMEM_LIMIT = 53 << 20


def solution(mesh):
    n_tm, n_tile = mesh.shape["tm"], mesh.shape["tile"]
    positions = n_tm * FRAMES * n_tile * ROWS * n_tile * STRIP
    return jax.shard_map(
        functools.partial(on_device, n_tm, n_tile, 1.0 / math.sqrt(positions)),
        mesh=mesh,
        in_specs=(P(None, "tile", "tm"), P("tm", None, "tile", None), P()),
        out_specs=(P("tm", None, "tile", None), P("tile", None)),
        check_vma=False,
    )
```

profile of v0, /device:TPU:1, one launch (start us, length us, event | category | flops | bytes accessed | tf_op | source)
XLA Modules:
  0.0 54.5 jit_solution(675017394780624876)
XLA Ops:
  0.6 41.2 %shard_map.50 = (bf16[8,160,8,512]{3,2,1,0:T(8,128)(2,1)S(1)}, f32[16,432]{1,0:T(8,128)S(1)}) custom-call(bf16[5,4,8,1024]{3,2,1,0:T(8,128)(2,1)} %bitcast.5, bf16[8,160,8,512]{3,2,1,0:T(8,128)(2,1)} %x_ref.1, bf16[432,512]{1,0:T(8,128)(2,1)} %bitcast.4), custom_call_target="tpu_custom_call" | custom-call | tf_op jit(solution)/shard_map/pallas_call | solution.py:470
  41.9 0.0 copy-start
  41.9 4.0 %copy-done = bf16[8,160,8,512]{3,2,1,0:T(8,128)(2,1)} copy-done((bf16[8,160,8,512]{3,2,1,0:T(8,128)(2,1)}, bf16[8,160,8,512]{3,2,1,0:T(8,128)(2,1)S(1)}, u32[]{:S(2)}) %copy-start) | copy-done | bytes 10485784
  45.8 0.0 copy-start.1
  45.8 0.6 %copy-done.1 = f32[16,432]{1,0:T(8,128)} copy-done((f32[16,432]{1,0:T(8,128)}, f32[16,432]{1,0:T(8,128)S(1)}, u32[]{:S(2)}) %copy-start.1) | copy-done | bytes 27672
  46.5 8.1 %shard_map.51 = (bf16[8,160,8,512]{3,2,1,0:T(8,128)(2,1)}, f32[16,432]{1,0:T(8,128)}) custom-call(bf16[8,160,8,512]{3,2,1,0:T(8,128)(2,1)} %copy-done, f32[16,432]{1,0:T(8,128)} %copy-done.1), custom_call_target="tpu_custom_call" | custom-call | tf_op jit(solution)/shard_map/pallas_call | solution.py:511
Async XLA Ops:
  41.9 4.0 %copy-start = (bf16[8,160,8,512]{3,2,1,0:T(8,128)(2,1)}, bf16[8,160,8,512]{3,2,1,0:T(8,128)(2,1)S(1)}, u32[]{:S(2)}) copy-start(bf16[8,160,8,512]{3,2,1,0:T(8,128)(2,1)S(1)} %get-tuple-element.4.grad_ref) | copy-start | bytes 31457284
  45.8 0.6 %copy-start.1 = (f32[16,432]{1,0:T(8,128)}, f32[16,432]{1,0:T(8,128)S(1)}, u32[]{:S(2)}) copy-start(f32[16,432]{1,0:T(8,128)S(1)} %get-tuple-element.5.kgrad_ref) | copy-start | bytes 82948
where the time goes:
time: 54.6 us; the launch traced here: 54.5 us
  Pallas kernels  49.3 us (90%)
  local copies, waits for them, and re-layouts  4.58 us (8%)
  between operations  0.65 us (1%)
    pallas_call x1, Pallas kernels, on_device(): pl.pallas_call(functools.partial(whole, n_tm, n_tile, scale), out_shape=(...  41.2 us
    pallas_call x1, Pallas kernels, on_device(): pl.pallas_call(write_out, out_shape=(jax.ShapeDtypeStruct((frames, height...  8.06 us
    unnamed x4, local copies, waits for them, and re-layouts  4.58 us

commit v1 on v0

--- a/solution.py
+++ b/solution.py
@@ -15,8 +15,8 @@
 STRIP = 8
 FRAMES = 8
 ROWS = 5
-FIRST = 5
-SECOND = 4
+FIRST = 4
+SECOND = 3
 EARLY = 4
 CORES = 2
 WINDOW = 3
@@ -52,15 +52,15 @@
     return rows[0] + rows[1] + rows[2] + rows[3], rows[4]
 
 
-def later_halo(first, second):
-    row = lane_of((FRAMES, 1), 0)
-    value = jnp.where(row < 6, turned(second, 4, 0), 0.0)
-    return jnp.where(row < 2, 0.0, jnp.where(row < 4, turned(first, 2, 0), value))
+def joined(upper, lower, turn_upper=False, turn_lower=False):
+    upper = turned(upper, EARLY, 0) if turn_upper else upper
+    lower = turned(lower, EARLY, 0) if turn_lower else lower
+    return jnp.where(lane_of((FRAMES, 1), 0) < EARLY, upper, lower)
 
 
 def whole(
     n_tm, n_tile, scale, grad_hbm, x_ref, kernel_hbm, out_ref, kgrad_ref,
-    grad_ref, kernel_ref, msg, msg_2, emsg, recv, recv_2, edge, act, slope, field, halo, vee, cols, cols_t, last, last_t,
+    grad_ref, kernel_ref, msg, msg_2, emsg, recv, recv_2, edge, lead, ahead, act, slope, field, halo, vee, cols, cols_t, last, last_t,
     weights, acc, part, mine, mine_half, pieces, sums, quads, in_sem, sems,
 ):
     frames, height, width, cin = out_ref.shape
@@ -78,6 +78,7 @@
     swap_send, swap_recv, piece_send, piece_recv = (sems.at[i] for i in range(4, 8))
     send_2, recv_main_2 = sems.at[10], sems.at[11]
     row_send, row_recv = sems.at[12], sems.at[13]
+    lead_send, lead_recv = sems.at[14], sems.at[15]
     core, y_lo = lax.rem(tm, CORES), tm // CORES
     groups = n_tile // CORES
     y_hi, spot = tile // groups, lax.rem(tile, groups)
@@ -119,6 +120,10 @@
         @pl.when(edge_block != tm)
         def _():
             hail(edge_block, tile)
+
+    @pl.when(tm < n_tm - 1)
+    def _():
+        hail(tm + 1, tile)
 
     hail(partner, tile)
     for k in range(1, groups):
@@ -147,22 +152,17 @@
         flipped.append(here)
         padded = [None, None] + here + [None, None]
         halos.append([strip_halo(padded[s], padded[s + 2]) for s in range(strips + 2)])
-    later = []
     for t in range(n_tm):
-        later.append([
-            nothing if t + 1 == n_tm else later_halo(*halos[t + 1][s]) for s in range(strips + 2)
-        ])
         for s in range(strips):
-            here = flipped[t][s]
+            here, (first, second) = flipped[t][s], halos[t][s + 1]
             tiles = [
-                jnp.where(row < EARLY, here[0], turned(here[1], EARLY, 0)),
-                jnp.where(row < EARLY, here[2], turned(here[3], EARLY, 0)),
-                here[4], *halos[t][s + 1],
+                joined(here[0], here[1], False, True), joined(here[2], here[3], False, True),
+                joined(here[4], first, False, True), joined(second, here[4]),
             ]
             for i, value in enumerate(tiles):
                 msg[t, s, i] = value.astype(BF16)
         for side, s in ((0, strips + 1), (1, 0)):
-            for i, value in enumerate([*halos[t][s], later[t][s]]):
+            for i, value in enumerate(halos[t][s]):
                 emsg[side, t, i] = value.astype(BF16)
 
     self_main = (block == tm).astype(jnp.int32)
@@ -175,7 +175,7 @@
     edges_out = n_tm * (to_right.astype(jnp.int32) + to_left.astype(jnp.int32))
     self_owner = (core == y_hi).astype(jnp.int32)
     exchange_out = messages - self_main + edges_out - self_edge
-    pl.semaphore_wait(barrier, exchange_out + 1 + groups - 1 + n_tm - self_owner)
+    pl.semaphore_wait(barrier, exchange_out + 1 + groups - 1 + n_tm - self_owner + to_left.astype(jnp.int32))
 
     def send(source, target, send_sem, recv_sem, target_tm, target_tile):
         own = is_me(target_tm, target_tile)
@@ -218,18 +218,9 @@
 
     for t in range(n_tm):
         for s in range(strips):
-            here, rest = flipped[t][s], later[t][s + 1]
-            if t + 1 < n_tm:
-                nxt = flipped[t + 1][s]
-                late = jnp.where(row < 6, turned(nxt[2], 4, 0), turned(nxt[3], 6, 0))
-                late = jnp.where(row < 2, nxt[0], jnp.where(row < 4, turned(nxt[1], 2, 0), late))
-                rest = jnp.where(row < 2, nxt[4], rest)
-            else:
-                late = nothing
+            here, (first, second) = flipped[t][s], halos[t][s + 1]
             tiles = [
-                jnp.where(row < EARLY, turned(here[0], EARLY, 0), here[1]),
-                jnp.where(row < EARLY, turned(here[2], EARLY, 0), here[3]),
-                late, rest,
+                joined(here[0], here[1], True), joined(here[2], here[3], True), joined(first, second, True),
             ]
             for i, value in enumerate(tiles):
                 msg_2[t, s, i] = value.astype(BF16)
@@ -274,28 +265,53 @@
 
     pltpu.make_async_copy(recv, recv, recv_main).wait()
 
+    def beside(value, i):
+        return turned(value, -OUT - 2 * OUT * i, 1)
+
     def unpack(b, _):
         tiles = [recv[b, i].astype(F32) for i in range(FIRST)]
-        beside = tiles[3] + edge[b, 0].astype(F32)
-        beside_4 = tiles[4] + edge[b, 1].astype(F32)
-        for i in range(ROWS):
-            at = b * ROWS + i
-            field[at, 0:FRAMES] = turned(tiles[i // 2], EARLY * (i % 2), 0)
-            halo[at, 0:FRAMES] = turned(beside if i < 4 else beside_4, -OUT - 2 * OUT * i, 1)
+        sides = turned(tiles[2], EARLY, 0) + edge[b, 0].astype(F32)
+        for i in range(ROWS - 1):
+            field[b * ROWS + i, 0:FRAMES] = turned(tiles[i // 2], EARLY * (i % 2), 0)
+            halo[b * ROWS + i, 0:FRAMES] = beside(sides, i)
+        field[b * ROWS + 4, 0:FRAMES] = joined(tiles[2], tiles[3])
+        halo[b * ROWS + 4, 0:FRAMES] = beside(tiles[3] + edge[b, 1].astype(F32), 4)
         return 0
 
     def unpack_2(b, _):
         tiles = [recv_2[b, i].astype(F32) for i in range(SECOND)]
-        late = tiles[3] + edge[b, 2].astype(F32)
-        for i in range(ROWS):
-            at = b * ROWS + i
-            if i < 4:
-                field[at, EARLY:FRAMES] = turned(tiles[i // 2], EARLY * (1 - i % 2), 0)[EARLY:]
-            field[at, FRAMES:] = turned(tiles[2], -2 * i, 0) if i < 4 else late
-            halo[at, FRAMES:] = turned(turned(late, -2 if i < 4 else -4, 0), -OUT - 2 * OUT * i, 1)
+        sides = turned(tiles[2], EARLY, 0) + edge[b, 0].astype(F32)
+        for i in range(ROWS - 1):
+            field[b * ROWS + i, EARLY:FRAMES] = turned(tiles[i // 2], EARLY * (1 - i % 2), 0)[EARLY:]
+            halo[b * ROWS + i, EARLY:FRAMES] = beside(sides, i)[EARLY:]
+        halo[b * ROWS + 4, EARLY:FRAMES] = beside(tiles[2] + edge[b, 1].astype(F32), 4)[EARLY:]
         return 0
 
     lax.fori_loop(0, n_tile, unpack, 0, unroll=4)
+
+    def pack_lead(k, _):
+        both = [
+            jnp.where(row < 2, field[2 * k + i, 0:FRAMES], turned(halo[2 * k + i, 0:FRAMES], 2, 0)) for i in range(2)
+        ]
+        lead[k] = joined(both[0], both[1], False, True).astype(BF16)
+        return 0
+
+    def unpack_ahead(k, _):
+        tiles = ahead[k].astype(F32)
+        for i in range(2):
+            field[2 * k + i, FRAMES:] = turned(tiles, -4 * i, 0)
+            halo[2 * k + i, FRAMES:] = turned(tiles, -4 * i - 2, 0)
+        return 0
+
+    lead_copy = pltpu.make_async_remote_copy(
+        src_ref=lead, dst_ref=ahead, send_sem=lead_send, recv_sem=lead_recv,
+        device_id=(jnp.maximum(tm - 1, 0), tile), device_id_type=MESH,
+    )
+
+    @pl.when(to_left)
+    def _():
+        lax.fori_loop(0, height // 2, pack_lead, 0, unroll=8)
+        lead_copy.start()
 
     lane3, col3 = lane_of((1, width, LANES), 2), lane_of((1, width, LANES), 1)
     outside = jnp.logical_or(
@@ -324,6 +340,16 @@
         if t == EARLY:
             pltpu.make_async_copy(recv_2, recv_2, recv_main_2).wait()
             lax.fori_loop(0, n_tile, unpack_2, 0, unroll=4)
+        if t == FRAMES:
+            @pl.when(to_right)
+            def _():
+                pltpu.make_async_copy(ahead, ahead, lead_recv).wait()
+
+            @pl.when(jnp.logical_not(to_right))
+            def _():
+                ahead[...] = jnp.zeros(ahead.shape, BF16)
+
+            lax.fori_loop(0, height // 2, unpack_ahead, 0, unroll=8)
 
         def spread(g, _, t=t):
             rows = pl.ds(g * group, group)
@@ -398,6 +424,10 @@
         return 0
 
     lax.fori_loop(0, edges_out - self_edge, drain_edge, 0)
+
+    @pl.when(to_left)
+    def _():
+        drain(lead, lead_send)
 
     rows = mine.shape[0]
     share = rows // groups
@@ -444,19 +474,7 @@
     kgrad_ref[...] = (result * scale)[:, : kgrad_ref.shape[1]]
 
 
-SPLIT = (1, 7)
-
-
-def write_out(grad_ref, kgrad_ref, grad_out, kgrad_out, sem):
-    frames, height = grad_ref.shape[:2]
-    copies = [pltpu.make_async_copy(kgrad_ref, kgrad_out, sem.at[2 * frames])]
-    for i in range(2 * frames):
-        place = (i // 2, pl.ds((i % 2) * (height // 2), height // 2))
-        copies.append(pltpu.make_async_copy(grad_ref.at[place], grad_out.at[place], sem.at[i]))
-    for copy in copies:
-        copy.start()
-    for copy in copies:
-        copy.wait()
+SPLIT = (1, 6)
 
 
 def on_device(n_tm, n_tile, scale, latent_grad, section_input, kernel):
@@ -467,7 +485,7 @@
     wide, count = frames + 2, height * width
     rows, share, padded = cin // CORES, cin // n_tile, 4 * LANES
     vmem = pl.BlockSpec(memory_space=pltpu.VMEM)
-    results = pl.pallas_call(
+    return pl.pallas_call(
         functools.partial(whole, n_tm, n_tile, scale),
         out_shape=(
             pltpu.VMEM((frames, height, width, cin), BF16),
@@ -480,10 +498,12 @@
             pltpu.VMEM((taps, cin), BF16),
             pltpu.VMEM((n_tm, strips, FIRST, FRAMES, LANES), BF16),
             pltpu.VMEM((n_tm, strips, SECOND, FRAMES, LANES), BF16),
-            pltpu.VMEM((2, n_tm, 3, FRAMES, LANES), BF16),
+            pltpu.VMEM((2, n_tm, 2, FRAMES, LANES), BF16),
             pltpu.VMEM((n_tile, FIRST, FRAMES, LANES), BF16),
             pltpu.VMEM((n_tile, SECOND, FRAMES, LANES), BF16),
-            pltpu.VMEM((n_tile, 3, FRAMES, LANES), BF16),
+            pltpu.VMEM((n_tile, 2, FRAMES, LANES), BF16),
+            pltpu.VMEM((height // 2, FRAMES, LANES), BF16),
+            pltpu.VMEM((height // 2, FRAMES, LANES), BF16),
             pltpu.VMEM((frames, count, cin), BF16),
             pltpu.VMEM((frames, count, cin), F32),
             pltpu.VMEM((height, 2 * FRAMES, LANES), F32),
@@ -508,16 +528,6 @@
             collective_id=0, has_side_effects=True, vmem_limit_bytes=VMEM_LIMIT
         ),
     )(banded, section_input, jnp.transpose(kernel))
-    return pl.pallas_call(
-        write_out,
-        out_shape=(
-            jax.ShapeDtypeStruct((frames, height, width, cin), BF16),
-            jax.ShapeDtypeStruct((share, taps), F32),
-        ),
-        in_specs=[vmem, vmem],
-        out_specs=[pl.BlockSpec(memory_space=pl.ANY)] * 2,
-        scratch_shapes=[pltpu.SemaphoreType.DMA((2 * frames + 1,))],
-    )(*results)
 
 
 VMEM_LIMIT = 53 << 20

time: 54.6 us -> 45.5 us (0.83)
  Pallas kernels: 49.3 us -> 40 us
    pallas_call x1 -> x0, Pallas kernels: 8.06 us -> none  [on_device(): pl.pallas_call(write_out, out_shape=(jax.ShapeDtypeStruct((frames, height...]
    pallas_call x1, Pallas kernels: 41.2 us -> 40 us  [on_device(): pl.pallas_call(functools.partial(whole, n_tm, n_tile, scale), out_shape=(...]
    unnamed x4 -> x2, local copies, waits for them, and re-layouts: 4.58 us -> 4.7 us
where the time goes in v1:
time: 45.5 us; the launch traced here: 45.4 us
  Pallas kernels  40 us (88%)
  local copies, waits for them, and re-layouts  4.7 us (10%)
  between operations  0.64 us (1%)
    pallas_call x1, Pallas kernels, on_device(): pl.pallas_call(functools.partial(whole, n_tm, n_tile, scale), out_shape=(...  40 us
    unnamed x2, local copies, waits for them, and re-layouts  4.7 us

profile of v1, /device:TPU:1, one launch (start us, length us, event | category | flops | bytes accessed | tf_op | source)
XLA Modules:
  0.0 45.4 jit_solution(3231850888742649904)
XLA Ops:
  0.6 40.0 %shard_map.50 = (bf16[8,160,8,512]{3,2,1,0:T(8,128)(2,1)S(1)}, f32[16,432]{1,0:T(8,128)S(1)}) custom-call(bf16[5,4,8,1024]{3,2,1,0:T(8,128)(2,1)} %bitcast.5, bf16[8,160,8,512]{3,2,1,0:T(8,128)(2,1)} %x_ref.1, bf16[432,512]{1,0:T(8,128)(2,1)} %bitcast.4), custom_call_target="tpu_custom_call" | custom-call | tf_op jit(solution)/shard_map/pallas_call | solution.py:488
  40.7 4.1 %copy.7 = bf16[8,160,8,512]{3,2,1,0:T(8,128)(2,1)} copy(bf16[8,160,8,512]{3,2,1,0:T(8,128)(2,1)S(1)} %get-tuple-element.2) | data formatting | bytes 20971520
  44.8 0.6 %copy.8 = f32[16,432]{1,0:T(8,128)} copy(f32[16,432]{1,0:T(8,128)S(1)} %get-tuple-element.3) | data formatting | bytes 55296

commit v2 on v1

--- a/solution.py
+++ b/solution.py
@@ -19,6 +19,7 @@
 SECOND = 3
 EARLY = 4
 CORES = 2
+KEPT = 4
 WINDOW = 3
 
 
@@ -61,7 +62,7 @@
 def whole(
     n_tm, n_tile, scale, grad_hbm, x_ref, kernel_hbm, out_ref, kgrad_ref,
     grad_ref, kernel_ref, msg, msg_2, emsg, recv, recv_2, edge, lead, ahead, act, slope, field, halo, vee, cols, cols_t, last, last_t,
-    weights, acc, part, mine, mine_half, pieces, sums, quads, in_sem, sems,
+    weights, acc, half, mine, pieces, sums, quads, in_sem, sems,
 ):
     frames, height, width, cin = out_ref.shape
     wide, count = frames + 2, height * width
@@ -75,10 +76,12 @@
     edge_block = jnp.where(place_in_block == 0, block - 1, block + 1)
     messages = n_tm * strips
     send_main, send_edge, recv_main, recv_edge = (sems.at[i] for i in range(4))
-    swap_send, swap_recv, piece_send, piece_recv = (sems.at[i] for i in range(4, 8))
     send_2, recv_main_2 = sems.at[10], sems.at[11]
-    row_send, row_recv = sems.at[12], sems.at[13]
-    lead_send, lead_recv = sems.at[14], sems.at[15]
+    lead_send, lead_recv = sems.at[12], sems.at[13]
+
+    def half_sem(kind, p):
+        return sems.at[14 + 2 * kind + p]
+
     core, y_lo = lax.rem(tm, CORES), tm // CORES
     groups = n_tile // CORES
     y_hi, spot = tile // groups, lax.rem(tile, groups)
@@ -235,25 +238,36 @@
 
     step = 8
 
-    def silu_frame(t, _):
+    def silu(x):
+        half_x = 0.5 * x.astype(F32).reshape(x.shape[0] * width, cin)
+        u = jnp.tanh(half_x)
+        more = 1.0 + u
+        value = half_x * more
+        return value, lambda: more + value * (1.0 - u)
+
+    def silu_frame(t, kept):
         fetch(t).wait()
 
         def silu_rows(r, _):
-            half_x = 0.5 * out_ref[t, pl.ds(r * step, step)].astype(F32).reshape(step * width, cin)
-            u = jnp.tanh(half_x)
-            more = 1.0 + u
-            value = half_x * more
+            value, slope_of = silu(out_ref[t, pl.ds(r * step, step)])
             rows = aligned(r, step * width)
             act[t, rows, :] = value.astype(BF16)
-            slope[t, rows, :] = more + value * (1.0 - u)
+            if kept:
+                slope[t, rows, :] = slope_of()
             return 0
 
         lax.fori_loop(0, height // step, silu_rows, 0, unroll=4)
-        return 0
-
-    lax.fori_loop(0, EARLY, silu_frame, 0)
+
+    def silu_frames(first, end, kept):
+        def one(t, _):
+            silu_frame(t, kept)
+            return 0
+
+        lax.fori_loop(first, end, one, 0)
+
+    silu_frames(0, KEPT, True)
     send_all(msg_2, recv_2, send_2, recv_main_2)
-    lax.fori_loop(EARLY, frames, silu_frame, 0)
+    silu_frames(KEPT, frames, False)
 
     @pl.when(jnp.logical_not(has_edge))
     def _():
@@ -331,10 +345,20 @@
         return turned(vee[t % WINDOW, at, :].astype(BF16), shift, 1)
 
     acc[...] = jnp.zeros(acc.shape, F32)
-
-    def add_frame(t):
-        left = jnp.concatenate([cols_t[t * LANES : (t + 3) * LANES, :], last_t[t]], axis=0)
-        acc[...] += jnp.dot(left, act[t], preferred_element_type=F32)
+    rest = LANES + 3 * OUT
+    half[1, rest:, :] = jnp.zeros((half.shape[1] - rest, half.shape[2]), F32)
+
+    def add_first(t):
+        grad = jnp.dot(cols_t[t * LANES : (t + 2) * LANES, :], act[t], preferred_element_type=F32)
+        for h in range(CORES):
+            acc[0, h] += grad[:, h * (cin // CORES) : (h + 1) * (cin // CORES)]
+
+    def add_second(t, _):
+        left = jnp.concatenate([cols_t[aligned(t + 2, LANES), :], last_t[t]], axis=0)
+        grad = jnp.dot(left, act[t], preferred_element_type=F32)
+        for h in range(CORES):
+            acc[1, h, 0:rest] += grad[:, h * (cin // CORES) : (h + 1) * (cin // CORES)]
+        return 0
 
     for t in range(wide):
         if t == EARLY:
@@ -379,29 +403,30 @@
         if t >= 2:
             lax.fori_loop(0, height // group, fill_last, 0, unroll=True)
             last_t[t - 2] = jnp.transpose(last[t - 2])[0 : 3 * OUT]
-        if t >= 3:
-            add_frame(t - 3)
-    add_frame(frames - 1)
-
-    pieces_of_total = []
-    for kt in range(3):
-        pieces_of_total.append(acc[kt * LANES : (kt + 1) * LANES, :])
-        pieces_of_total.append(acc[3 * LANES + kt * OUT : 3 * LANES + (kt + 1) * OUT, :])
-    pieces_of_total.append(jnp.zeros((part.shape[1] - 27 * OUT, cin), F32))
-    part[...] = jnp.transpose(jnp.concatenate(pieces_of_total, axis=0))
+        if t >= 2:
+            add_first(t - 2)
 
     chunk = 40
 
-    def grad_frame(t, _):
+    def grad_frame(t, kept):
         def grad_rows(r, _):
             rows = aligned(r, chunk * width)
             left = jnp.concatenate([cols[t + kt, rows, :] for kt in range(3)] + [last[t, rows, :]], axis=1)
-            grad = jnp.dot(left, weights[...], preferred_element_type=F32) * slope[t, rows, :]
+            grad = jnp.dot(left, weights[...], preferred_element_type=F32)
+            grad = grad * (slope[t, rows, :] if kept else silu(out_ref[t, pl.ds(r * chunk, chunk)])[1]())
             out_ref[t, pl.ds(r * chunk, chunk)] = grad.reshape(chunk, width, cin).astype(BF16)
             return 0
 
         lax.fori_loop(0, height // chunk, grad_rows, 0, unroll=True)
-        return 0
+
+    def grad_frames(first, end):
+        for kept, a, b in ((True, first, min(end, KEPT)), (False, max(first, KEPT), end)):
+            def one(t, _, kept=kept):
+                grad_frame(t, kept)
+                return 0
+
+            if a < b:
+                lax.fori_loop(a, b, one, 0)
 
     def drain(source, sem):
         pltpu.make_async_copy(source, source, sem).wait()
@@ -429,52 +454,69 @@
     def _():
         drain(lead, lead_send)
 
-    rows = mine.shape[0]
-    share = rows // groups
-    swap = pltpu.make_async_remote_copy(
-        src_ref=part.at[aligned(1 - core, rows)], dst_ref=mine,
-        send_sem=swap_send, recv_sem=swap_recv,
-        device_id=(partner, tile), device_id_type=MESH,
-    )
-    swap.start()
-    lax.fori_loop(0, SPLIT[0], grad_frame, 0)
-    swap.wait()
-    mine[...] += part[aligned(core, rows), :]
-
-    mine_half[...] = mine[...].astype(BF16)
-
-    for k in range(1, groups):
-        g = wrapped(spot + k, groups)
-        pltpu.make_async_remote_copy(
-            src_ref=mine_half.at[aligned(g, share)], dst_ref=pieces.at[spot],
-            send_sem=piece_send, recv_sem=piece_recv,
-            device_id=(tm, y_hi * groups + g), device_id_type=MESH,
-        ).start()
-    pieces[spot] = mine_half[aligned(spot, share), :]
-    lax.fori_loop(SPLIT[0], SPLIT[1], grad_frame, 0)
-    others = pieces.at[pl.ds(0, groups - 1)]
-    pltpu.make_async_copy(others, others, piece_recv).wait()
-    sums[...] = jnp.sum(pieces[...].astype(F32), axis=0)
-
-    for k in range(n_tm):
-        send(sums, quads.at[level], row_send, row_recv, k, owner_tile)
-    lax.fori_loop(SPLIT[1], frames, grad_frame, 0)
-    pltpu.make_async_copy(quads, quads, row_recv).wait()
-
-    drain(others, piece_send)
-    drain(quads.at[pl.ds(0, n_tm - 1)], row_send)
+    share = mine.shape[1] // groups
+    used = (acc.shape[2], rest)
+
+    def swap(p):
+        return pltpu.make_async_remote_copy(
+            src_ref=acc.at[p, 1 - core, pl.ds(0, used[p])], dst_ref=half.at[p, pl.ds(0, used[p])],
+            send_sem=half_sem(0, p), recv_sem=half_sem(1, p),
+            device_id=(partner, tile), device_id_type=MESH,
+        )
+
+    def send_pieces(p):
+        swap(p).wait()
+        mine[p] = jnp.transpose(acc[p, core] + half[p]).astype(BF16)
+        for k in range(1, groups):
+            g = wrapped(spot + k, groups)
+            pltpu.make_async_remote_copy(
+                src_ref=mine.at[p, aligned(g, share)], dst_ref=pieces.at[p, spot],
+                send_sem=half_sem(2, p), recv_sem=half_sem(3, p),
+                device_id=(tm, y_hi * groups + g), device_id_type=MESH,
+            ).start()
+        pieces[p, spot] = mine[p, aligned(spot, share), :]
+
+    def send_sums(p):
+        drain(pieces.at[p, pl.ds(0, groups - 1)], half_sem(3, p))
+        sums[p] = jnp.sum(pieces[p].astype(F32), axis=0)
+        for k in range(n_tm):
+            send(sums.at[p], quads.at[p, level], half_sem(4, p), half_sem(5, p), k, owner_tile)
+
+    swap(0).start()
+    lax.fori_loop(0, frames, add_second, 0)
+    swap(1).start()
+    send_pieces(0)
+    grad_frames(0, SPLIT[0])
+    send_pieces(1)
+    grad_frames(SPLIT[0], SPLIT[1])
+    send_sums(0)
+    grad_frames(SPLIT[1], SPLIT[2])
+    send_sums(1)
+    grad_frames(SPLIT[2], frames)
+
+    results = []
+    for p in range(2):
+        drain(quads.at[p], half_sem(5, p))
+        drain(pieces.at[p, pl.ds(0, groups - 1)], half_sem(2, p))
+        drain(quads.at[p, pl.ds(0, n_tm - 1)], half_sem(4, p))
+        result = quads[p, 0]
+        for k in range(1, n_tm):
+            result = result + quads[p, k]
+        results.append(result * scale)
 
     @pl.when(core != y_hi)
     def _():
-        drain(sums, row_send)
-
-    result = quads[0]
-    for k in range(1, n_tm):
-        result = result + quads[k]
-    kgrad_ref[...] = (result * scale)[:, : kgrad_ref.shape[1]]
-
-
-SPLIT = (1, 6)
+        for p in range(2):
+            drain(sums.at[p], half_sem(4, p))
+
+    blocks = [results[0][:, :LANES], results[0][:, LANES:], results[1][:, :LANES]]
+    for kt in range(3):
+        at = 9 * kt * OUT
+        kgrad_ref[:, at : at + LANES] = blocks[kt]
+        kgrad_ref[:, at + LANES : at + 9 * OUT] = results[1][:, LANES + kt * OUT : LANES + (kt + 1) * OUT]
+
+
+SPLIT = (1, 4, 5)
 
 
 def on_device(n_tm, n_tile, scale, latent_grad, section_input, kernel):
@@ -505,7 +547,7 @@
             pltpu.VMEM((height // 2, FRAMES, LANES), BF16),
             pltpu.VMEM((height // 2, FRAMES, LANES), BF16),
             pltpu.VMEM((frames, count, cin), BF16),
-            pltpu.VMEM((frames, count, cin), F32),
+            pltpu.VMEM((KEPT, count, cin), F32),
             pltpu.VMEM((height, 2 * FRAMES, LANES), F32),
             pltpu.VMEM((height, 2 * FRAMES, LANES), F32),
             pltpu.VMEM((WINDOW, (height + 2) * width, LANES), F32),
@@ -514,15 +556,14 @@
             pltpu.VMEM((frames, count, LANES), BF16),
             pltpu.VMEM((frames, 3 * OUT, count), BF16),
             pltpu.VMEM((padded, cin), BF16),
-            pltpu.VMEM((27 * OUT, cin), F32),
-            pltpu.VMEM((cin, padded), F32),
-            pltpu.VMEM((rows, padded), F32),
-            pltpu.VMEM((rows, padded), BF16),
-            pltpu.VMEM((n_tile // CORES, share, padded), BF16),
-            pltpu.VMEM((share, padded), F32),
-            pltpu.VMEM((n_tm, share, padded), F32),
+            pltpu.VMEM((2, CORES, 2 * LANES, rows), F32),
+            pltpu.VMEM((2, 2 * LANES, rows), F32),
+            pltpu.VMEM((2, rows, 2 * LANES), BF16),
+            pltpu.VMEM((2, n_tile // CORES, share, 2 * LANES), BF16),
+            pltpu.VMEM((2, share, 2 * LANES), F32),
+            pltpu.VMEM((2, n_tm, share, 2 * LANES), F32),
             pltpu.SemaphoreType.DMA((frames,)),
-            pltpu.SemaphoreType.DMA((16,)),
+            pltpu.SemaphoreType.DMA((26,)),
         ],
         compiler_params=pltpu.CompilerParams(
             collective_id=0, has_side_effects=True, vmem_limit_bytes=VMEM_LIMIT

time: 45.5 us -> 46.1 us (1.013)
  Pallas kernels: 40 us -> 40.6 us
    pallas_call x1, Pallas kernels: 40 us -> 40.6 us  [on_device(): pl.pallas_call(functools.partial(whole, n_tm, n_tile, scale), out_shape=(...]
where the time goes in v2:
time: 46.1 us; the launch traced here: 45.9 us
  Pallas kernels  40.6 us (88%)
  local copies, waits for them, and re-layouts  4.7 us (10%)
  between operations  0.64 us (1%)
    pallas_call x1, Pallas kernels, on_device(): pl.pallas_call(functools.partial(whole, n_tm, n_tile, scale), out_shape=(...  40.6 us
    unnamed x2, local copies, waits for them, and re-layouts  4.7 us

profile of v2, /device:TPU:1, one launch (start us, length us, event | category | flops | bytes accessed | tf_op | source)
XLA Modules:
  0.0 45.9 jit_solution(11105236915181183261)
XLA Ops:
  0.6 40.6 %shard_map.50 = (bf16[8,160,8,512]{3,2,1,0:T(8,128)(2,1)S(1)}, f32[16,432]{1,0:T(8,128)S(1)}) custom-call(bf16[5,4,8,1024]{3,2,1,0:T(8,128)(2,1)} %bitcast.5, bf16[8,160,8,512]{3,2,1,0:T(8,128)(2,1)} %x_ref.1, bf16[432,512]{1,0:T(8,128)(2,1)} %bitcast.4), custom_call_target="tpu_custom_call" | custom-call | tf_op jit(solution)/shard_map/pallas_call | solution.py:530
  41.2 4.1 %copy.7 = bf16[8,160,8,512]{3,2,1,0:T(8,128)(2,1)} copy(bf16[8,160,8,512]{3,2,1,0:T(8,128)(2,1)S(1)} %get-tuple-element.2) | data formatting | bytes 20971520
  45.3 0.6 %copy.8 = f32[16,432]{1,0:T(8,128)} copy(f32[16,432]{1,0:T(8,128)S(1)} %get-tuple-element.3) | data formatting | bytes 55296

commit v3 on v2

--- a/solution.py
+++ b/solution.py
@@ -19,7 +19,6 @@
 SECOND = 3
 EARLY = 4
 CORES = 2
-KEPT = 4
 WINDOW = 3
 
 
@@ -205,19 +204,21 @@
 
         return 0
 
-    def send_all(source, target, send_sem, recv_sem):
-        for k in range(messages):
-            t, s = wrapped(tm + k // strips, n_tm), wrapped(place_in_block + k % strips, strips)
-            if k == 0:
-                send(source.at[t, s], target.at[tile], send_sem, recv_sem, t, tm * strips + s)
-            else:
-                pltpu.make_async_remote_copy(
-                    src_ref=source.at[t, s], dst_ref=target.at[tile], send_sem=send_sem, recv_sem=recv_sem,
-                    device_id=(t, tm * strips + s), device_id_type=MESH,
-                ).start()
+    def send_away(source, target, send_sem, recv_sem, k):
+        t = wrapped(tm + lax.div(k, strips), n_tm)
+        s = wrapped(place_in_block + lax.rem(k, strips), strips)
+        pltpu.make_async_remote_copy(
+            src_ref=source.at[t, s], dst_ref=target.at[tile], send_sem=send_sem, recv_sem=recv_sem,
+            device_id=(t, tm * strips + s), device_id_type=MESH,
+        ).start()
+
+    def send_first(source, target, send_sem, recv_sem):
+        send(source.at[tm, place_in_block], target.at[tile], send_sem, recv_sem, tm, tm * strips + place_in_block)
 
     lax.fori_loop(0, n_tm, send_edges, 0)
-    send_all(msg, recv, send_main, recv_main)
+    send_first(msg, recv, send_main, recv_main)
+    for k in range(1, messages):
+        send_away(msg, recv, send_main, recv_main, jnp.int32(k))
 
     for t in range(n_tm):
         for s in range(strips):
@@ -243,31 +244,39 @@
         u = jnp.tanh(half_x)
         more = 1.0 + u
         value = half_x * more
-        return value, lambda: more + value * (1.0 - u)
-
-    def silu_frame(t, kept):
-        fetch(t).wait()
-
-        def silu_rows(r, _):
-            value, slope_of = silu(out_ref[t, pl.ds(r * step, step)])
-            rows = aligned(r, step * width)
-            act[t, rows, :] = value.astype(BF16)
-            if kept:
-                slope[t, rows, :] = slope_of()
+        return value, more + value * (1.0 - u)
+
+    def silu_rows(t, r):
+        value, slope_here = silu(out_ref[t, pl.ds(r * step, step)])
+        rows = aligned(r, step * width)
+        act[t, rows, :] = value.astype(BF16)
+        slope[t, rows, :] = slope_here
+
+    steps = height // step
+    bunch = 4 if steps % 4 == 0 else 1
+
+    def silu_frames(first, end, sends):
+        def one(t, _):
+            fetch(t).wait()
+
+            def some(i, _):
+                for k in range(sends):
+                    send_away(msg_2, recv_2, send_2, recv_main_2, 1 + sends * ((t - first) * (steps // bunch) + i) + k)
+                for k in range(bunch):
+                    silu_rows(t, i * bunch + k)
+                return 0
+
+            lax.fori_loop(0, steps // bunch, some, 0)
             return 0
 
-        lax.fori_loop(0, height // step, silu_rows, 0, unroll=4)
-
-    def silu_frames(first, end, kept):
-        def one(t, _):
-            silu_frame(t, kept)
-            return 0
-
         lax.fori_loop(first, end, one, 0)
 
-    silu_frames(0, KEPT, True)
-    send_all(msg_2, recv_2, send_2, recv_main_2)
-    silu_frames(KEPT, frames, False)
+    sending = (messages - 1) // (2 * (steps // bunch))
+    send_first(msg_2, recv_2, send_2, recv_main_2)
+    silu_frames(0, sending, 2)
+    for k in range(1 + 2 * sending * (steps // bunch), messages):
+        send_away(msg_2, recv_2, send_2, recv_main_2, jnp.int32(k))
+    silu_frames(sending, frames, 0)
 
     @pl.when(jnp.logical_not(has_edge))
     def _():
@@ -332,17 +341,10 @@
         jnp.logical_and(col3 == 0, lane3 < OUT),
         jnp.logical_and(col3 == width - 1, lane3 >= LANES - OUT),
     )
-    edge_rows = jnp.zeros((width, LANES), F32)
-    group = 16
-    for t in range(WINDOW):
-        vee[t, 0:width, :] = edge_rows
-        vee[t, (height + 1) * width : (height + 2) * width, :] = edge_rows
+    edge_row = jnp.zeros((width, LANES), F32)
+    group = 32
 
     lane2 = lane_of((1, LANES), 1)
-
-    def tap(t, g, shift_rows, shift):
-        at = pl.ds(pl.multiple_of((g * group + shift_rows) * width, width), group * width)
-        return turned(vee[t % WINDOW, at, :].astype(BF16), shift, 1)
 
     acc[...] = jnp.zeros(acc.shape, F32)
     rest = LANES + 3 * OUT
@@ -375,58 +377,53 @@
 
             lax.fori_loop(0, height // 2, unpack_ahead, 0, unroll=8)
 
-        def spread(g, _, t=t):
-            rows = pl.ds(g * group, group)
-            main = jnp.broadcast_to(field[rows, t : t + 1, :], (group, width, LANES))
-            side = jnp.broadcast_to(halo[rows, t : t + 1, :], (group, width, LANES))
-            at = pl.ds(pl.multiple_of((g * group + 1) * width, width), group * width)
-            values = jnp.where(outside, side, main).reshape(group * width, LANES)
-            vee[t % WINDOW, at, :] = pltpu.roll(values, 0, 1, stride=OUT, stride_axis=0)
-            return 0
-
-        def fill(g, _, t=t):
-            rows = aligned(g, group * width)
-            s0, s1, s2 = tap(t, g, 2, 2 * OUT), tap(t, g, 1, 5 * OUT), tap(t, g, 0, 0)
-            cols[t, rows, :] = jnp.where(lane2 < 3 * OUT, s0, jnp.where(lane2 < 6 * OUT, s1, s2))
-            return 0
-
-        def fill_last(g, _, t=t):
-            rows = aligned(g, group * width)
-            taps = [tap(t - 2 + kt, g, 0, kt * OUT) for kt in range(3)]
-            value = jnp.where(lane2 < 3 * OUT, taps[2], jnp.zeros_like(taps[2]))
-            last[t - 2, rows, :] = jnp.where(lane2 < OUT, taps[0], jnp.where(lane2 < 2 * OUT, taps[1], value))
-            return 0
-
-        lax.fori_loop(0, height // group, spread, 0, unroll=True)
-        lax.fori_loop(0, height // group, fill, 0, unroll=True)
+        for g in range(height // group):
+            first, end = max(g * group - 1, 0), min((g + 1) * group + 1, height)
+            main = jnp.broadcast_to(field[first:end, t : t + 1, :], (end - first, width, LANES))
+            side = jnp.broadcast_to(halo[first:end, t : t + 1, :], (end - first, width, LANES))
+            values = jnp.where(outside, side, main).reshape((end - first) * width, LANES)
+            values = pltpu.roll(values, 0, 1, stride=OUT, stride_axis=0)
+            if g == 0:
+                values = jnp.concatenate([edge_row, values], axis=0)
+            if end == height:
+                values = jnp.concatenate([values, edge_row], axis=0)
+            size = group * width
+            rows = slice(g * size, (g + 1) * size)
+            around = values.astype(BF16)
+            inside = values[width : width + size].astype(BF16)
+            ahead_turned = pltpu.roll(around, 2 * OUT, 1)
+            before = around[:size]
+            cols[t, rows, :] = jnp.where(
+                lane2 < 3 * OUT, ahead_turned[2 * width :],
+                jnp.where(lane2 < 6 * OUT, pltpu.roll(inside, 5 * OUT, 1), before),
+            )
+            vee[t % WINDOW, rows, :] = before
+            if t >= 2:
+                value = jnp.where(lane2 < 3 * OUT, ahead_turned[:size], jnp.zeros_like(before))
+                value = jnp.where(lane2 < 2 * OUT, pltpu.roll(vee[(t - 1) % WINDOW, rows, :], OUT, 1), value)
+                last[t - 2, rows, :] = jnp.where(lane2 < OUT, vee[(t - 2) % WINDOW, rows, :], value)
         cols_t[t * LANES : (t + 1) * LANES, :] = jnp.transpose(cols[t])
         if t >= 2:
-            lax.fori_loop(0, height // group, fill_last, 0, unroll=True)
             last_t[t - 2] = jnp.transpose(last[t - 2])[0 : 3 * OUT]
         if t >= 2:
             add_first(t - 2)
 
     chunk = 40
 
-    def grad_frame(t, kept):
+    def grad_frame(t, _):
         def grad_rows(r, _):
             rows = aligned(r, chunk * width)
             left = jnp.concatenate([cols[t + kt, rows, :] for kt in range(3)] + [last[t, rows, :]], axis=1)
             grad = jnp.dot(left, weights[...], preferred_element_type=F32)
-            grad = grad * (slope[t, rows, :] if kept else silu(out_ref[t, pl.ds(r * chunk, chunk)])[1]())
+            grad = grad * slope[t, rows, :]
             out_ref[t, pl.ds(r * chunk, chunk)] = grad.reshape(chunk, width, cin).astype(BF16)
             return 0
 
         lax.fori_loop(0, height // chunk, grad_rows, 0, unroll=True)
+        return 0
 
     def grad_frames(first, end):
-        for kept, a, b in ((True, first, min(end, KEPT)), (False, max(first, KEPT), end)):
-            def one(t, _, kept=kept):
-                grad_frame(t, kept)
-                return 0
-
-            if a < b:
-                lax.fori_loop(a, b, one, 0)
+        lax.fori_loop(first, end, grad_frame, 0)
 
     def drain(source, sem):
         pltpu.make_async_copy(source, source, sem).wait()
@@ -547,10 +544,10 @@
             pltpu.VMEM((height // 2, FRAMES, LANES), BF16),
             pltpu.VMEM((height // 2, FRAMES, LANES), BF16),
             pltpu.VMEM((frames, count, cin), BF16),
-            pltpu.VMEM((KEPT, count, cin), F32),
+            pltpu.VMEM((frames, count, cin), F32),
             pltpu.VMEM((height, 2 * FRAMES, LANES), F32),
             pltpu.VMEM((height, 2 * FRAMES, LANES), F32),
-            pltpu.VMEM((WINDOW, (height + 2) * width, LANES), F32),
+            pltpu.VMEM((WINDOW, count, LANES), BF16),
             pltpu.VMEM((wide, count, LANES), BF16),
             pltpu.VMEM((wide * LANES, count), BF16),
             pltpu.VMEM((frames, count, LANES), BF16),

time: 46.1 us -> 48 us (1.041)
  Pallas kernels: 40.6 us -> 42.5 us
    pallas_call x1, Pallas kernels: 40.6 us -> 42.5 us  [on_device(): pl.pallas_call(functools.partial(whole, n_tm, n_tile, scale), out_shape=(...]
where the time goes in v3:
time: 48 us; the launch traced here: 47.9 us
  Pallas kernels  42.5 us (89%)
  local copies, waits for them, and re-layouts  4.7 us (10%)
  between operations  0.64 us (1%)
    pallas_call x1, Pallas kernels, on_device(): pl.pallas_call(functools.partial(whole, n_tm, n_tile, scale), out_shape=(...  42.5 us
    unnamed x2, local copies, waits for them, and re-layouts  4.7 us

profile of v3, /device:TPU:1, one launch (start us, length us, event | category | flops | bytes accessed | tf_op | source)
XLA Modules:
  0.0 47.9 jit_solution(2759138745790009594)
XLA Ops:
  0.6 42.5 %shard_map.50 = (bf16[8,160,8,512]{3,2,1,0:T(8,128)(2,1)S(1)}, f32[16,432]{1,0:T(8,128)S(1)}) custom-call(bf16[5,4,8,1024]{3,2,1,0:T(8,128)(2,1)} %bitcast.5, bf16[8,160,8,512]{3,2,1,0:T(8,128)(2,1)} %x_ref.1, bf16[432,512]{1,0:T(8,128)(2,1)} %bitcast.4), custom_call_target="tpu_custom_call" | custom-call | tf_op jit(solution)/shard_map/pallas_call | solution.py:527
  43.2 4.1 %copy.7 = bf16[8,160,8,512]{3,2,1,0:T(8,128)(2,1)} copy(bf16[8,160,8,512]{3,2,1,0:T(8,128)(2,1)S(1)} %get-tuple-element.2) | data formatting | bytes 20971520
  47.3 0.6 %copy.8 = f32[16,432]{1,0:T(8,128)} copy(f32[16,432]{1,0:T(8,128)S(1)} %get-tuple-element.3) | data formatting | bytes 55296

commit v4 on v1

--- a/solution.py
+++ b/solution.py
@@ -19,6 +19,7 @@
 SECOND = 3
 EARLY = 4
 CORES = 2
+KEPT = 4
 WINDOW = 3
 
 
@@ -235,25 +236,33 @@
 
     step = 8
 
-    def silu_frame(t, _):
-        fetch(t).wait()
-
-        def silu_rows(r, _):
-            half_x = 0.5 * out_ref[t, pl.ds(r * step, step)].astype(F32).reshape(step * width, cin)
-            u = jnp.tanh(half_x)
-            more = 1.0 + u
-            value = half_x * more
-            rows = aligned(r, step * width)
-            act[t, rows, :] = value.astype(BF16)
-            slope[t, rows, :] = more + value * (1.0 - u)
+    def silu(x):
+        half_x = 0.5 * x.astype(F32).reshape(x.shape[0] * width, cin)
+        u = jnp.tanh(half_x)
+        more = 1.0 + u
+        value = half_x * more
+        return value, lambda: more + value * (1.0 - u)
+
+    def silu_frames(first, end, kept):
+        def one(t, _):
+            fetch(t).wait()
+
+            def silu_rows(r, _):
+                value, slope_of = silu(out_ref[t, pl.ds(r * step, step)])
+                rows = aligned(r, step * width)
+                act[t, rows, :] = value.astype(BF16)
+                if kept:
+                    slope[t, rows, :] = slope_of()
+                return 0
+
+            lax.fori_loop(0, height // step, silu_rows, 0, unroll=4)
             return 0
 
-        lax.fori_loop(0, height // step, silu_rows, 0, unroll=4)
-        return 0
-
-    lax.fori_loop(0, EARLY, silu_frame, 0)
+        lax.fori_loop(first, end, one, 0)
+
+    silu_frames(0, KEPT, True)
     send_all(msg_2, recv_2, send_2, recv_main_2)
-    lax.fori_loop(EARLY, frames, silu_frame, 0)
+    silu_frames(KEPT, frames, False)
 
     @pl.when(jnp.logical_not(has_edge))
     def _():
@@ -392,16 +401,25 @@
 
     chunk = 40
 
-    def grad_frame(t, _):
+    def grad_frame(t, kept):
         def grad_rows(r, _):
             rows = aligned(r, chunk * width)
             left = jnp.concatenate([cols[t + kt, rows, :] for kt in range(3)] + [last[t, rows, :]], axis=1)
-            grad = jnp.dot(left, weights[...], preferred_element_type=F32) * slope[t, rows, :]
+            grad = jnp.dot(left, weights[...], preferred_element_type=F32)
+            grad = grad * (slope[t, rows, :] if kept else silu(out_ref[t, pl.ds(r * chunk, chunk)])[1]())
             out_ref[t, pl.ds(r * chunk, chunk)] = grad.reshape(chunk, width, cin).astype(BF16)
             return 0
 
         lax.fori_loop(0, height // chunk, grad_rows, 0, unroll=True)
-        return 0
+
+    def grad_frames(first, end):
+        for kept, a, b in ((True, first, min(end, KEPT)), (False, max(first, KEPT), end)):
+            def one(t, _, kept=kept):
+                grad_frame(t, kept)
+                return 0
+
+            if a < b:
+                lax.fori_loop(a, b, one, 0)
 
     def drain(source, sem):
         pltpu.make_async_copy(source, source, sem).wait()
@@ -437,7 +455,7 @@
         device_id=(partner, tile), device_id_type=MESH,
     )
     swap.start()
-    lax.fori_loop(0, SPLIT[0], grad_frame, 0)
+    grad_frames(0, SPLIT[0])
     swap.wait()
     mine[...] += part[aligned(core, rows), :]
 
@@ -451,14 +469,14 @@
             device_id=(tm, y_hi * groups + g), device_id_type=MESH,
         ).start()
     pieces[spot] = mine_half[aligned(spot, share), :]
-    lax.fori_loop(SPLIT[0], SPLIT[1], grad_frame, 0)
+    grad_frames(SPLIT[0], SPLIT[1])
     others = pieces.at[pl.ds(0, groups - 1)]
     pltpu.make_async_copy(others, others, piece_recv).wait()
     sums[...] = jnp.sum(pieces[...].astype(F32), axis=0)
 
     for k in range(n_tm):
         send(sums, quads.at[level], row_send, row_recv, k, owner_tile)
-    lax.fori_loop(SPLIT[1], frames, grad_frame, 0)
+    grad_frames(SPLIT[1], frames)
     pltpu.make_async_copy(quads, quads, row_recv).wait()
 
     drain(others, piece_send)
@@ -505,7 +523,7 @@
             pltpu.VMEM((height // 2, FRAMES, LANES), BF16),
             pltpu.VMEM((height // 2, FRAMES, LANES), BF16),
             pltpu.VMEM((frames, count, cin), BF16),
-            pltpu.VMEM((frames, count, cin), F32),
+            pltpu.VMEM((KEPT, count, cin), F32),
             pltpu.VMEM((height, 2 * FRAMES, LANES), F32),
             pltpu.VMEM((height, 2 * FRAMES, LANES), F32),
             pltpu.VMEM((WINDOW, (height + 2) * width, LANES), F32),

time: 45.5 us -> 45.7 us (level)
  no operation moved by 1% of the time
where the time goes in v4:
time: 45.7 us; the launch traced here: 45.6 us
  Pallas kernels  40.2 us (88%)
  local copies, waits for them, and re-layouts  4.7 us (10%)
  between operations  0.64 us (1%)
    pallas_call x1, Pallas kernels, on_device(): pl.pallas_call(functools.partial(whole, n_tm, n_tile, scale), out_shape=(...  40.2 us
    unnamed x2, local copies, waits for them, and re-layouts  4.7 us

profile of v4, /device:TPU:1, one launch (start us, length us, event | category | flops | bytes accessed | tf_op | source)
XLA Modules:
  0.0 45.6 jit_solution(5164270860820851582)
XLA Ops:
  0.6 40.2 %shard_map.50 = (bf16[8,160,8,512]{3,2,1,0:T(8,128)(2,1)S(1)}, f32[16,432]{1,0:T(8,128)S(1)}) custom-call(bf16[5,4,8,1024]{3,2,1,0:T(8,128)(2,1)} %bitcast.5, bf16[8,160,8,512]{3,2,1,0:T(8,128)(2,1)} %x_ref.1, bf16[432,512]{1,0:T(8,128)(2,1)} %bitcast.4), custom_call_target="tpu_custom_call" | custom-call | tf_op jit(solution)/shard_map/pallas_call | solution.py:506
  40.9 4.1 %copy.7 = bf16[8,160,8,512]{3,2,1,0:T(8,128)(2,1)} copy(bf16[8,160,8,512]{3,2,1,0:T(8,128)(2,1)S(1)} %get-tuple-element.2) | data formatting | bytes 20971520
  45.0 0.6 %copy.8 = f32[16,432]{1,0:T(8,128)} copy(f32[16,432]{1,0:T(8,128)S(1)} %get-tuple-element.3) | data formatting | bytes 55296

commit v5 on v1

--- a/solution.py
+++ b/solution.py
@@ -141,18 +141,55 @@
     row = lane_of((FRAMES, 1), 0)
     nothing = jnp.zeros((FRAMES, LANES), F32)
     grad_copy.wait()
+    rows = [grad_ref[:, t].astype(F32).reshape(ROWS * FRAMES, strips * LANES) for t in range(n_tm)]
+    rows = jnp.concatenate(
+        [rows[t][:, s * LANES : (s + 1) * LANES] for t in range(n_tm) for s in range(strips)], axis=0
+    )
+    rows = jnp.dot(rows.astype(BF16), flip, preferred_element_type=F32).reshape(n_tm, strips, ROWS, FRAMES, LANES)
     flipped, halos = [], []
     for t in range(n_tm):
-        rows = grad_ref[:, t].astype(F32).reshape(ROWS * FRAMES, strips * LANES).astype(BF16)
-        here = [
-            jnp.dot(rows[:, s * LANES : (s + 1) * LANES], flip, preferred_element_type=F32)
-            .reshape(ROWS, FRAMES, LANES)
-            for s in range(strips)
-        ]
+        here = [rows[t, s] for s in range(strips)]
         flipped.append(here)
         padded = [None, None] + here + [None, None]
         halos.append([strip_halo(padded[s], padded[s + 2]) for s in range(strips + 2)])
-    for t in range(n_tm):
+    self_main = (block == tm).astype(jnp.int32)
+    to_right, to_left = tm < n_tm - 1, tm > 0
+    right_tile, left_tile = (tm + 1) * strips, tm * strips - 1
+    self_edge = (
+        jnp.logical_and(to_right, tile == right_tile).astype(jnp.int32)
+        + jnp.logical_and(to_left, tile == left_tile).astype(jnp.int32)
+    )
+    edges_out = n_tm * (to_right.astype(jnp.int32) + to_left.astype(jnp.int32))
+    self_owner = (core == y_hi).astype(jnp.int32)
+    exchange_out = messages - self_main + edges_out - self_edge
+    all_here = (exchange_out + 1 + groups - 1 + n_tm - self_owner + to_left.astype(jnp.int32))
+
+    def send(source, target, send_sem, recv_sem, target_tm, target_tile):
+        own = is_me(target_tm, target_tile)
+
+        @pl.when(jnp.logical_not(own))
+        def _():
+            pltpu.make_async_remote_copy(
+                src_ref=source, dst_ref=target, send_sem=send_sem, recv_sem=recv_sem,
+                device_id=(target_tm, target_tile), device_id_type=MESH,
+            ).start()
+
+        @pl.when(own)
+        def _():
+            pltpu.make_async_copy(source, target, recv_sem).start()
+
+    def send_block(source, target, send_sem, recv_sem, t):
+        for k in range(strips):
+            s = wrapped(place_in_block + k, strips)
+            if k == 0:
+                send(source.at[t, s], target.at[tile], send_sem, recv_sem, t, tm * strips + s)
+            else:
+                pltpu.make_async_remote_copy(
+                    src_ref=source.at[t, s], dst_ref=target.at[tile], send_sem=send_sem, recv_sem=recv_sem,
+                    device_id=(t, tm * strips + s), device_id_type=MESH,
+                ).start()
+
+    def make_block(t):
         for s in range(strips):
             here, (first, second) = flipped[t][s], halos[t][s + 1]
             tiles = [
@@ -165,33 +202,9 @@
             for i, value in enumerate(halos[t][s]):
                 emsg[side, t, i] = value.astype(BF16)
 
-    self_main = (block == tm).astype(jnp.int32)
-    to_right, to_left = tm < n_tm - 1, tm > 0
-    right_tile, left_tile = (tm + 1) * strips, tm * strips - 1
-    self_edge = (
-        jnp.logical_and(to_right, tile == right_tile).astype(jnp.int32)
-        + jnp.logical_and(to_left, tile == left_tile).astype(jnp.int32)
-    )
-    edges_out = n_tm * (to_right.astype(jnp.int32) + to_left.astype(jnp.int32))
-    self_owner = (core == y_hi).astype(jnp.int32)
-    exchange_out = messages - self_main + edges_out - self_edge
-    pl.semaphore_wait(barrier, exchange_out + 1 + groups - 1 + n_tm - self_owner + to_left.astype(jnp.int32))
-
-    def send(source, target, send_sem, recv_sem, target_tm, target_tile):
-        own = is_me(target_tm, target_tile)
-
-        @pl.when(jnp.logical_not(own))
-        def _():
-            pltpu.make_async_remote_copy(
-                src_ref=source, dst_ref=target, send_sem=send_sem, recv_sem=recv_sem,
-                device_id=(target_tm, target_tile), device_id_type=MESH,
-            ).start()
-
-        @pl.when(own)
-        def _():
-            pltpu.make_async_copy(source, target, recv_sem).start()
-
-    def send_edges(t, _):
+    def leave_block(t):
+        send_block(msg, recv, send_main, recv_main, t)
+
         @pl.when(to_right)
         def _():
             send(emsg.at[0, t], edge.at[tile], send_edge, recv_edge, t, right_tile)
@@ -200,21 +213,14 @@
         def _():
             send(emsg.at[1, t], edge.at[tile], send_edge, recv_edge, t, left_tile)
 
-        return 0
-
-    def send_all(source, target, send_sem, recv_sem):
-        for k in range(messages):
-            t, s = wrapped(tm + k // strips, n_tm), wrapped(place_in_block + k % strips, strips)
-            if k == 0:
-                send(source.at[t, s], target.at[tile], send_sem, recv_sem, t, tm * strips + s)
-            else:
-                pltpu.make_async_remote_copy(
-                    src_ref=source.at[t, s], dst_ref=target.at[tile], send_sem=send_sem, recv_sem=recv_sem,
-                    device_id=(t, tm * strips + s), device_id_type=MESH,
-                ).start()
-
-    lax.fori_loop(0, n_tm, send_edges, 0)
-    send_all(msg, recv, send_main, recv_main)
+    ready = n_tm // 2
+    for t in range(ready):
+        make_block(t)
+    pl.semaphore_wait(barrier, all_here)
+    for t in range(n_tm):
+        leave_block(t)
+        if ready + t < n_tm:
+            make_block(ready + t)
 
     for t in range(n_tm):
         for s in range(strips):
@@ -252,7 +258,8 @@
         return 0
 
     lax.fori_loop(0, EARLY, silu_frame, 0)
-    send_all(msg_2, recv_2, send_2, recv_main_2)
+    for t in range(n_tm):
+        send_block(msg_2, recv_2, send_2, recv_main_2, t)
     lax.fori_loop(EARLY, frames, silu_frame, 0)
 
     @pl.when(jnp.logical_not(has_edge))

time: 45.5 us -> 45 us (0.989)
  Pallas kernels: 40 us -> 39.5 us
    pallas_call x1, Pallas kernels: 40 us -> 39.5 us  [on_device(): pl.pallas_call(functools.partial(whole, n_tm, n_tile, scale), out_shape=(...]
where the time goes in v5:
time: 45 us; the launch traced here: 44.9 us
  Pallas kernels  39.5 us (88%)
  local copies, waits for them, and re-layouts  4.7 us (10%)
  between operations  0.64 us (1%)
    pallas_call x1, Pallas kernels, on_device(): pl.pallas_call(functools.partial(whole, n_tm, n_tile, scale), out_shape=(...  39.5 us
    unnamed x2, local copies, waits for them, and re-layouts  4.7 us

profile of v5, /device:TPU:1, one launch (start us, length us, event | category | flops | bytes accessed | tf_op | source)
XLA Modules:
  0.0 44.9 jit_solution(11024285987550015475)
XLA Ops:
  0.6 39.5 %shard_map.50 = (bf16[8,160,8,512]{3,2,1,0:T(8,128)(2,1)S(1)}, f32[16,432]{1,0:T(8,128)S(1)}) custom-call(bf16[5,4,8,1024]{3,2,1,0:T(8,128)(2,1)} %bitcast.5, bf16[8,160,8,512]{3,2,1,0:T(8,128)(2,1)} %x_ref.1, bf16[432,512]{1,0:T(8,128)(2,1)} %bitcast.4), custom_call_target="tpu_custom_call" | custom-call | tf_op jit(solution)/shard_map/pallas_call | solution.py:495
  40.2 4.1 %copy.7 = bf16[8,160,8,512]{3,2,1,0:T(8,128)(2,1)} copy(bf16[8,160,8,512]{3,2,1,0:T(8,128)(2,1)S(1)} %get-tuple-element.2) | data formatting | bytes 20971520
  44.3 0.6 %copy.8 = f32[16,432]{1,0:T(8,128)} copy(f32[16,432]{1,0:T(8,128)S(1)} %get-tuple-element.3) | data formatting | bytes 55296

commit v6 on v5

--- a/solution.py
+++ b/solution.py
@@ -61,7 +61,7 @@
 def whole(
     n_tm, n_tile, scale, grad_hbm, x_ref, kernel_hbm, out_ref, kgrad_ref,
     grad_ref, kernel_ref, msg, msg_2, emsg, recv, recv_2, edge, lead, ahead, act, slope, field, halo, vee, cols, cols_t, last, last_t,
-    weights, acc, part, mine, mine_half, pieces, sums, quads, in_sem, sems,
+    weights, acc, half, mine_half, pieces, sums, quads, in_sem, sems,
 ):
     frames, height, width, cin = out_ref.shape
     wide, count = frames + 2, height * width
@@ -339,11 +339,15 @@
 
     acc[...] = jnp.zeros(acc.shape, F32)
 
-    def add_frame(t):
-        left = jnp.concatenate([cols_t[t * LANES : (t + 3) * LANES, :], last_t[t]], axis=0)
-        acc[...] += jnp.dot(left, act[t], preferred_element_type=F32)
+    def add_frames(t):
+        left = jnp.concatenate([
+            jnp.concatenate([cols_t[i * LANES : (i + 3) * LANES, :], last_t[i]], axis=0) for i in (t, t + 1)
+        ], axis=1)
+        acc[...] += jnp.dot(left, act[t : t + 2].reshape(2 * count, cin), preferred_element_type=F32)
 
     for t in range(wide):
+        if t >= 4 and t % 2 == 0:
+            add_frames(t - 4)
         if t == EARLY:
             pltpu.make_async_copy(recv_2, recv_2, recv_main_2).wait()
             lax.fori_loop(0, n_tile, unpack_2, 0, unroll=4)
@@ -386,16 +390,16 @@
         if t >= 2:
             lax.fori_loop(0, height // group, fill_last, 0, unroll=True)
             last_t[t - 2] = jnp.transpose(last[t - 2])[0 : 3 * OUT]
-        if t >= 3:
-            add_frame(t - 3)
-    add_frame(frames - 1)
-
-    pieces_of_total = []
-    for kt in range(3):
-        pieces_of_total.append(acc[kt * LANES : (kt + 1) * LANES, :])
-        pieces_of_total.append(acc[3 * LANES + kt * OUT : 3 * LANES + (kt + 1) * OUT, :])
-    pieces_of_total.append(jnp.zeros((part.shape[1] - 27 * OUT, cin), F32))
-    part[...] = jnp.transpose(jnp.concatenate(pieces_of_total, axis=0))
+    add_frames(frames - 2)
+
+    rows = half.shape[1]
+    share = rows // groups
+    swap = pltpu.make_async_remote_copy(
+        src_ref=acc.at[:, aligned(1 - core, rows)], dst_ref=half,
+        send_sem=swap_send, recv_sem=swap_recv,
+        device_id=(partner, tile), device_id_type=MESH,
+    )
+    swap.start()
 
     chunk = 40
 
@@ -410,6 +414,9 @@
         lax.fori_loop(0, height // chunk, grad_rows, 0, unroll=True)
         return 0
 
+    def grad_frames(first, end):
+        lax.fori_loop(first, end, grad_frame, 0)
+
     def drain(source, sem):
         pltpu.make_async_copy(source, source, sem).wait()
 
@@ -436,19 +443,15 @@
     def _():
         drain(lead, lead_send)
 
-    rows = mine.shape[0]
-    share = rows // groups
-    swap = pltpu.make_async_remote_copy(
-        src_ref=part.at[aligned(1 - core, rows)], dst_ref=mine,
-        send_sem=swap_send, recv_sem=swap_recv,
-        device_id=(partner, tile), device_id_type=MESH,
-    )
-    swap.start()
-    lax.fori_loop(0, SPLIT[0], grad_frame, 0)
+    grad_frames(0, SPLIT[0])
     swap.wait()
-    mine[...] += part[aligned(core, rows), :]
-
-    mine_half[...] = mine[...].astype(BF16)
+    own = acc[:, aligned(core, rows)] + half[...]
+    ordered = []
+    for kt in range(3):
+        ordered.append(own[kt * LANES : (kt + 1) * LANES])
+        ordered.append(own[3 * LANES + kt * OUT : 3 * LANES + (kt + 1) * OUT])
+    ordered.append(jnp.zeros((mine_half.shape[1] - 27 * OUT, rows), F32))
+    mine_half[...] = jnp.transpose(jnp.concatenate(ordered, axis=0)).astype(BF16)
 
     for k in range(1, groups):
         g = wrapped(spot + k, groups)
@@ -458,14 +461,14 @@
             device_id=(tm, y_hi * groups + g), device_id_type=MESH,
         ).start()
     pieces[spot] = mine_half[aligned(spot, share), :]
-    lax.fori_loop(SPLIT[0], SPLIT[1], grad_frame, 0)
+    grad_frames(SPLIT[0], SPLIT[1])
     others = pieces.at[pl.ds(0, groups - 1)]
     pltpu.make_async_copy(others, others, piece_recv).wait()
     sums[...] = jnp.sum(pieces[...].astype(F32), axis=0)
 
     for k in range(n_tm):
         send(sums, quads.at[level], row_send, row_recv, k, owner_tile)
-    lax.fori_loop(SPLIT[1], frames, grad_frame, 0)
+    grad_frames(SPLIT[1], frames)
     pltpu.make_async_copy(quads, quads, row_recv).wait()
 
     drain(others, piece_send)
@@ -522,8 +525,7 @@
             pltpu.VMEM((frames, 3 * OUT, count), BF16),
             pltpu.VMEM((padded, cin), BF16),
             pltpu.VMEM((27 * OUT, cin), F32),
-            pltpu.VMEM((cin, padded), F32),
-            pltpu.VMEM((rows, padded), F32),
+            pltpu.VMEM((27 * OUT, rows), F32),
             pltpu.VMEM((rows, padded), BF16),
             pltpu.VMEM((n_tile // CORES, share, padded), BF16),
             pltpu.VMEM((share, padded), F32),

time: 45 us -> 47.3 us (1.051)
  Pallas kernels: 39.5 us -> 41.8 us
    pallas_call x1, Pallas kernels: 39.5 us -> 41.8 us  [on_device(): pl.pallas_call(functools.partial(whole, n_tm, n_tile, scale), out_shape=(...]
where the time goes in v6:
time: 47.3 us; the launch traced here: 47.2 us
  Pallas kernels  41.8 us (88%)
  local copies, waits for them, and re-layouts  4.7 us (10%)
  between operations  0.64 us (1%)
    pallas_call x1, Pallas kernels, on_device(): pl.pallas_call(functools.partial(whole, n_tm, n_tile, scale), out_shape=(...  41.8 us
    unnamed x2, local copies, waits for them, and re-layouts  4.7 us

profile of v6, /device:TPU:1, one launch (start us, length us, event | category | flops | bytes accessed | tf_op | source)
XLA Modules:
  0.0 47.2 jit_solution(2043005666356966890)
XLA Ops:
  0.6 41.8 %shard_map.50 = (bf16[8,160,8,512]{3,2,1,0:T(8,128)(2,1)S(1)}, f32[16,432]{1,0:T(8,128)S(1)}) custom-call(bf16[5,4,8,1024]{3,2,1,0:T(8,128)(2,1)} %bitcast.5, bf16[8,160,8,512]{3,2,1,0:T(8,128)(2,1)} %x_ref.1, bf16[432,512]{1,0:T(8,128)(2,1)} %bitcast.4), custom_call_target="tpu_custom_call" | custom-call | tf_op jit(solution)/shard_map/pallas_call | solution.py:498
  42.5 4.1 %copy.7 = bf16[8,160,8,512]{3,2,1,0:T(8,128)(2,1)} copy(bf16[8,160,8,512]{3,2,1,0:T(8,128)(2,1)S(1)} %get-tuple-element.2) | data formatting | bytes 20971520
  46.5 0.6 %copy.8 = f32[16,432]{1,0:T(8,128)} copy(f32[16,432]{1,0:T(8,128)S(1)} %get-tuple-element.3) | data formatting | bytes 55296

commit v7 on v5

--- a/solution.py
+++ b/solution.py
@@ -254,7 +254,7 @@
             slope[t, rows, :] = more + value * (1.0 - u)
             return 0
 
-        lax.fori_loop(0, height // step, silu_rows, 0, unroll=4)
+        lax.fori_loop(0, height // step, silu_rows, 0, unroll=10)
         return 0
 
     lax.fori_loop(0, EARLY, silu_frame, 0)
@@ -294,7 +294,7 @@
         halo[b * ROWS + 4, EARLY:FRAMES] = beside(tiles[2] + edge[b, 1].astype(F32), 4)[EARLY:]
         return 0
 
-    lax.fori_loop(0, n_tile, unpack, 0, unroll=4)
+    lax.fori_loop(0, n_tile, unpack, 0, unroll=8)
 
     def pack_lead(k, _):
         both = [
@@ -346,7 +346,7 @@
     for t in range(wide):
         if t == EARLY:
             pltpu.make_async_copy(recv_2, recv_2, recv_main_2).wait()
-            lax.fori_loop(0, n_tile, unpack_2, 0, unroll=4)
+            lax.fori_loop(0, n_tile, unpack_2, 0, unroll=8)
         if t == FRAMES:
             @pl.when(to_right)
             def _():

time: 45 us -> 44.4 us (0.987)
  Pallas kernels: 39.5 us -> 39 us
    pallas_call x1, Pallas kernels: 39.5 us -> 39 us  [on_device(): pl.pallas_call(functools.partial(whole, n_tm, n_tile, scale), out_shape=(...]
where the time goes in v7:
time: 44.4 us; the launch traced here: 44.3 us
  Pallas kernels  39 us (88%)
  local copies, waits for them, and re-layouts  4.7 us (11%)
  between operations  0.64 us (1%)
    pallas_call x1, Pallas kernels, on_device(): pl.pallas_call(functools.partial(whole, n_tm, n_tile, scale), out_shape=(...  39 us
    unnamed x2, local copies, waits for them, and re-layouts  4.7 us

profile of v7, /device:TPU:1, one launch (start us, length us, event | category | flops | bytes accessed | tf_op | source)
XLA Modules:
  0.0 44.3 jit_solution(4493722170943275472)
XLA Ops:
  0.6 39.0 %shard_map.50 = (bf16[8,160,8,512]{3,2,1,0:T(8,128)(2,1)S(1)}, f32[16,432]{1,0:T(8,128)S(1)}) custom-call(bf16[5,4,8,1024]{3,2,1,0:T(8,128)(2,1)} %bitcast.5, bf16[8,160,8,512]{3,2,1,0:T(8,128)(2,1)} %x_ref.1, bf16[432,512]{1,0:T(8,128)(2,1)} %bitcast.4), custom_call_target="tpu_custom_call" | custom-call | tf_op jit(solution)/shard_map/pallas_call | solution.py:495
  39.6 4.1 %copy.7 = bf16[8,160,8,512]{3,2,1,0:T(8,128)(2,1)} copy(bf16[8,160,8,512]{3,2,1,0:T(8,128)(2,1)S(1)} %get-tuple-element.2) | data formatting | bytes 20971520
  43.7 0.6 %copy.8 = f32[16,432]{1,0:T(8,128)} copy(f32[16,432]{1,0:T(8,128)S(1)} %get-tuple-element.3) | data formatting | bytes 55296

commit v8 on v7

--- a/solution.py
+++ b/solution.py
@@ -341,7 +341,9 @@
 
     def add_frame(t):
         left = jnp.concatenate([cols_t[t * LANES : (t + 3) * LANES, :], last_t[t]], axis=0)
-        acc[...] += jnp.dot(left, act[t], preferred_element_type=F32)
+        for i in range(2):
+            some = slice(i * (count // 2), (i + 1) * (count // 2))
+            acc[...] += jnp.dot(left[:, some], act[t, some, :], preferred_element_type=F32)
 
     for t in range(wide):
         if t == EARLY:

time: 44.4 us -> 44.8 us (level)
  no operation moved by 1% of the time
where the time goes in v8:
time: 44.8 us; the launch traced here: 44.7 us
  Pallas kernels  39.3 us (88%)
  local copies, waits for them, and re-layouts  4.7 us (10%)
  between operations  0.64 us (1%)
    pallas_call x1, Pallas kernels, on_device(): pl.pallas_call(functools.partial(whole, n_tm, n_tile, scale), out_shape=(...  39.3 us
    unnamed x2, local copies, waits for them, and re-layouts  4.7 us

profile of v8, /device:TPU:1, one launch (start us, length us, event | category | flops | bytes accessed | tf_op | source)
XLA Modules:
  0.0 44.7 jit_solution(7648267450449805689)
XLA Ops:
  0.6 39.3 %shard_map.50 = (bf16[8,160,8,512]{3,2,1,0:T(8,128)(2,1)S(1)}, f32[16,432]{1,0:T(8,128)S(1)}) custom-call(bf16[5,4,8,1024]{3,2,1,0:T(8,128)(2,1)} %bitcast.5, bf16[8,160,8,512]{3,2,1,0:T(8,128)(2,1)} %x_ref.1, bf16[432,512]{1,0:T(8,128)(2,1)} %bitcast.4), custom_call_target="tpu_custom_call" | custom-call | tf_op jit(solution)/shard_map/pallas_call | solution.py:497
  40.0 4.1 %copy.7 = bf16[8,160,8,512]{3,2,1,0:T(8,128)(2,1)} copy(bf16[8,160,8,512]{3,2,1,0:T(8,128)(2,1)S(1)} %get-tuple-element.2) | data formatting | bytes 20971520
  44.1 0.6 %copy.8 = f32[16,432]{1,0:T(8,128)} copy(f32[16,432]{1,0:T(8,128)S(1)} %get-tuple-element.3) | data formatting | bytes 55296
